TPU v7x, 128 devices: a whole 4x4x4 slice. The times are simulated.
128 devices in a mesh: dp: 16 (over x_hi, z, core), tensor: 8 (over x_lo, y).
Axes of the slice: x: 4 (x_hi: 2, x_lo: 2; x = x_hi * 2 + x_lo), y: 4, z: 4, core: 2. Of those that a mesh axis runs over, the one named last changes fastest.
Arguments:
- activations: bfloat16 [8192, 14336], P('dp', 'tensor'), may hold values from -6 to 6
- output_grads: bfloat16 [8192, 4096], P('dp', 'tensor'), may hold values from -6 to 6
- basis_in: float32 [16, 896, 896], P('dp'), may hold values from -0.1875 to 0.1875
- eigen_in: float32 [14336], P('dp'), may hold values from 0.1 to 1
- basis_out: float32 [4096, 512], P('tensor'), may hold values from -0.25 to 0.25
- eigen_out: float32 [4096], P('tensor'), may hold values from 0.1 to 1
Outputs:
- update: bfloat16 [14336, 4096], P(None, 'tensor')
- factor_in: float32 [896, 16, 896], P('dp', 'tensor')
- factor_out: float32 [512, 4096], P('dp', 'tensor')
All inputs are finite; a program needn't handle non-finite values.
Results may differ from a plain program's by a relative error of at most 0.019.
Values may be sent and summed in bfloat16 or wider, within the bound.
A program may use at most 128 MiB of HBM per device.

v0:
```python
import jax
import jax.numpy as jnp
from jax import lax
from jax.sharding import PartitionSpec as P

BLK = 896


damping = 0.01


def contract_rows(left, right):
    return lax.dot_general(
        left, right, (((0,), (0,)), ((), ())), preferred_element_type=jnp.float32
    )


def reduce_input_factor(local_blocks, total_tokens):
    return lax.psum_scatter(
        (
            jnp.einsum(
                "tbi,tbj->ibj", local_blocks, local_blocks, preferred_element_type=jnp.float32
            )
            / total_tokens
        ).astype(jnp.bfloat16),
        "dp",
        scatter_dimension=0,
        tiled=True,
    ).astype(jnp.float32)


def body(activations, output_grads, basis_in, eigen_in, basis_out, eigen_out):
    highest = lax.Precision.HIGHEST
    replicas = lax.axis_size("dp")
    tok_rows = activations.shape[0]
    total_tokens = tok_rows * replicas
    rows_slab = output_grads.shape[1]
    blocks_local = activations.shape[1] // BLK
    local_blocks = activations.reshape(tok_rows, blocks_local, BLK)
    whole = lax.all_gather(activations, "tensor", axis=1, tiled=True)
    factor_in = reduce_input_factor(local_blocks, total_tokens)
    part = whole
    grad_cols = lax.psum_scatter(
        (contract_rows(part, output_grads) / total_tokens).astype(jnp.bfloat16),
        "dp",
        scatter_dimension=0,
        tiled=True,
    ).astype(jnp.float32)
    part = output_grads
    factor_out = lax.psum_scatter(
        (contract_rows(part, output_grads) / total_tokens).astype(jnp.bfloat16),
        "dp",
        scatter_dimension=0,
        tiled=True,
    ).astype(jnp.float32)
    block_count = basis_in.shape[0]
    blocked = grad_cols.reshape(block_count, BLK, rows_slab)
    values_in = eigen_in.reshape(block_count, BLK)
    rotated = jnp.einsum("bij,bik->bjk", basis_in, blocked, precision=highest)
    rotated = jnp.einsum("bjk,kl->bjl", rotated, basis_out, precision=highest)
    scaled = rotated / (values_in[:, :, None] * eigen_out[None, None, :] + damping)
    back = jnp.einsum("bjl,bij->bil", scaled, basis_in, precision=highest)
    back = jnp.einsum("bil,kl->bik", back, basis_out, precision=highest)
    worker_slab = back.reshape(block_count * BLK, rows_slab).astype(jnp.bfloat16)
    update = lax.all_gather(worker_slab, "dp", axis=0, tiled=True)
    return (update, factor_in, factor_out)


def solution(mesh):
    in_specs = (
        P("dp", "tensor"),
        P("dp", "tensor"),
        P("dp", None, None),
        P("dp"),
        P("tensor", None),
        P("tensor"),
    )
    out_specs = (P(None, "tensor"), P("dp", "tensor", None), P("dp", "tensor"))
    return jax.shard_map(body, mesh=mesh, in_specs=in_specs, out_specs=out_specs, check_vma=False)
```

profile of v0, /device:TPU:1, one launch (start us, length us, event | category | flops | bytes accessed | tf_op | source)
XLA Modules:
  0.0 650.3 jit_solution(11697579030822750949)
XLA Ops:
  7.2 0.0 copy-start
  7.2 0.0 all-gather.3.cloned.1.call-start
  7.2 0.7 all-gather.3.cloned.1.call-update
  7.9 0.0 reduce-scatter.3.cloned.1.call-start
  8.0 155.8 %all-gather.3.cloned.1.call-done = bf16[512,14336]{1,0:T(8,128)(2,1)} async-done(((bf16[512,1792]{1,0:T(8,128)(2,1)}), bf16[512,14336]{1,0:T(8,128)(2,1)}) %all-gather.3.cloned.1.call-update) | async-done | bytes 14680080 | tf_op jit(solution)/shard_map/all_gather | solution.py:40
  163.8 14.3 %multiply_convert_fusion = bf16[14336,512]{1,0:T(8,128)(2,1)} fusion(bf16[512,14336]{1,0:T(8,128)(2,1)} %all-gather.3.cloned.1.call-done, bf16[512,512]{1,0:T(8,128)(2,1)} %param.7), kind=kOutput, calls=%fused_computation | convolution fusion | flops 7530872832 | bytes 29884416 | tf_op jit(solution)/shard_map/dot_general | solution.py:13
  178.1 0.0 reduce-scatter.3.cloned.1.call-update
  178.1 0.0 reduce-scatter.5.cloned.1.call-start
  178.1 2.5 fusion.10
  180.6 0.0 reduce-scatter.5.cloned.1.call-update
  180.7 0.0 all-reduce.3.cloned.1.call-start
  180.7 5.8 fusion
  186.6 10.4 %copy.14 = bf16[896,2,896]{2,1,0:T(2,128)(2,1)} copy(bf16[896,2,896]{0,2,1:T(8,128)(2,1)} %fusion) | data formatting | bytes 6422528 | tf_op jit(solution)/shard_map/convert_element_type | solution.py:25
  196.9 0.0 all-reduce.3.cloned.1.call-update
  196.9 0.2 all-gather.5.cloned.1.call-start
  197.2 112.0 %reduce-scatter.3.cloned.1.call-done = bf16[896,512]{1,0:T(8,128)(2,1)} async-done(((bf16[14336,512]{1,0:T(8,128)(2,1)}), bf16[896,512]{1,0:T(8,128)(2,1)}) %reduce-scatter.3.cloned.1.call-update) | async-done | bytes 917520 | tf_op jit(solution)/shard_map/reduce_scatter | solution.py:43
  309.1 0.0 copy-done
  309.1 0.0 copy-start.1
  309.1 4.7 fusion.3
  313.8 0.0 copy-done.1
  313.9 0.0 copy-start.2
  313.9 0.0 copy-start.3
  313.9 3.1 fusion.15
  317.0 0.0 copy-done.2
  317.0 0.0 copy-done.3
  317.0 12.2 %fusion.1 = f32[512,896]{1,0:T(8,128)S(1)} fusion(f32[1,896,896]{2,1,0:T(8,128)S(1)} %copy-done, f32[896,512]{1,0:T(8,128)S(1)} %fusion.15, f32[512]{0:T(512)S(1)} %copy-done.3, f32[896]{0:T(1024)S(1)} %copy-done.2), kind=kOutput, calls=%fused_computation.3 | convolution fusion | flops 4933877760 | bytes 6886912 | tf_op jit(solution)/shard_map/bjl,bij->bil/dot_general | solution.py:62
  329.2 0.0 copy-start.4
  329.2 7.0 %convolution_convert_fusion = bf16[896,512]{1,0:T(8,128)(2,1)} fusion(f32[512,896]{1,0:T(8,128)S(1)} %fusion.1, f32[512,512]{1,0:T(8,128)S(1)} %copy-done.1), kind=kOutput, calls=%fused_computation.12 | convolution fusion | flops 2819031040 | bytes 3801088 | tf_op jit(solution)/shard_map/bil,kl->bik/dot_general | solution.py:63
  336.1 0.0 all-gather.5.cloned.1.call-update
  336.2 0.0 copy-done.4
  336.2 0.6 dynamic-slice
  337.4 37.7 %reduce-scatter.5.cloned.1.call-done = bf16[32,512]{1,0:T(8,128)(2,1)} async-done(((bf16[512,512]{1,0:T(8,128)(2,1)}), bf16[32,512]{1,0:T(8,128)(2,1)}) %reduce-scatter.5.cloned.1.call-update) | async-done | bytes 32784 | tf_op jit(solution)/shard_map/reduce_scatter | solution.py:50
  375.1 1.4 convert_element_type.28
  376.5 149.4 %all-reduce.3.cloned.1.call-done = bf16[896,2,896]{2,1,0:T(2,128)(2,1)} async-done(((bf16[896,2,896]{2,1,0:T(2,128)(2,1)}), bf16[896,2,896]{2,1,0:T(2,128)(2,1)}) %all-reduce.3.cloned.1.call-update) | async-done | bytes 3211280
  525.9 1.8 dynamic-slice_convert_fusion
  527.7 102.9 %all-gather.5.cloned.1.call-done = bf16[14336,512]{1,0:T(8,128)(2,1)} async-done(((bf16[896,512]{1,0:T(8,128)(2,1)}), bf16[14336,512]{1,0:T(8,128)(2,1)}) %all-gather.5.cloned.1.call-update) | async-done | bytes 14680080 | tf_op jit(solution)/shard_map/all_gather | solution.py:65
  630.7 13.1 %copy.22 = bf16[14336,512]{1,0:T(8,128)(2,1)} copy(bf16[14336,512]{1,0:T(8,128)(2,1)} %all-gather.5.cloned.1.call-done) | data formatting | bytes 29360128
Async XLA Ops:
  7.2 302.0 %copy-start = (f32[1,896,896]{2,1,0:T(8,128)S(1)}, f32[1,896,896]{2,1,0:T(8,128)}, u32[]{:S(2)}) copy-start(f32[1,896,896]{2,1,0:T(8,128)} %param.8) | copy-start | bytes 9633796
  7.2 156.6 %all-gather.3.cloned.1.call-start = ((), (), s32[]{:S(2)}) async-start(), calls=%async_computation.2 | async-start | bytes 16515072 | tf_op jit(solution)/shard_map/all_gather | solution.py:40
  7.9 301.2 %reduce-scatter.3.cloned.1.call-start = ((), (), s32[]{:S(2)}) async-start(), calls=%async_computation.3 | async-start | bytes 15597568 | tf_op jit(solution)/shard_map/reduce_scatter | solution.py:43
  178.1 197.0 %reduce-scatter.5.cloned.1.call-start = ((), (), s32[]{:S(2)}) async-start(), calls=%async_computation.5 | async-start | bytes 557056 | tf_op jit(solution)/shard_map/reduce_scatter | solution.py:50
  180.7 345.2 %all-reduce.3.cloned.1.call-start = ((), (), s32[]{:S(2)}) async-start(), calls=%async_computation.6 | async-start | bytes 6422528
  196.9 433.7 %all-gather.5.cloned.1.call-start = ((), (), s32[]{:S(2)}) async-start(), calls=%async_computation.4 | async-start | bytes 15597568 | tf_op jit(solution)/shard_map/all_gather | solution.py:65
  309.1 4.7 copy-start.1
  313.9 3.1 copy-start.2
  313.9 3.1 copy-start.3
  329.2 7.0 %copy-start.4 = (u32[128]{0:T(128)S(1)}, u32[128]{0:T(128)}, u32[]{:S(2)}) copy-start(u32[128]{0:T(128)} %constant.12) | copy-start | bytes 1540
Sparse Core Ops, SparseCore 0:
  9.7 154.0 all-gather.2
  178.2 130.8 reduce-scatter.2
  312.8 62.1 reduce-scatter.4
  377.6 148.2 all-reduce.2
  529.1 101.4 all-gather.4
where the time goes:
time: 651 us; the launch traced here: 650 us
  waiting for transfers between devices  559 us (86%)
  matrix products  49.6 us (8%)
  local copies, waits for them, and re-layouts  24.1 us (4%)
  between operations  14.5 us (2%)
    all_gather x1, waiting for transfers between devices, body(): whole = lax.all_gather(activations, 'tensor', axis=1, tiled=True)  156 us
    unnamed x6, waiting for transfers between devices  150 us
    reduce_scatter x2, waiting for transfers between devices, body(): lax.psum_scatter((contract_rows(part, output_grads) / total_tokens).astyp...  150 us
    all_gather x1, waiting for transfers between devices, body(): update = lax.all_gather(worker_slab, 'dp', axis=0, tiled=True)  103 us
    dot_general x2, matrix products, contract_rows(): lax.dot_general(left, right, (((0,), (0,)), ((), ())), preferred_element_...  16.8 us
    unnamed x12, local copies, waits for them, and re-layouts  13.7 us
  transfers between devices with their start and end apart: 5, of which 5 were waited for; matrix products, arithmetic and copies ran while one was open for 8% of the time, Pallas kernels for 0%

commit v1 on v0

v1 whole, which is shorter than its diff:
```python
import functools
import jax
import jax.numpy as jnp
from jax import lax
from jax.experimental import pallas as pl
from jax.experimental.pallas import tpu as pltpu
from jax.sharding import PartitionSpec as P

MESH = pl.DeviceIdType.MESH
BLK = 896
ROWS = 512
TOK = 512
NP = 7
PW = 128
SCALE = 1.0 / 8192
damping = 0.01
f32, bf16 = jnp.float32, jnp.bfloat16


def where():
    dp, t = lax.axis_index("dp"), lax.axis_index("tensor")
    return dp // 8, t // 4, t % 4, (dp // 2) % 4, dp % 2


def device(xh, xl, y, z, c):
    return (xh * 8 + (z % 4) * 2 + c, xl * 4 + (y % 4))


def contract0(a, b):
    return lax.dot_general(a, b, (((0,), (0,)), ((), ())), preferred_element_type=f32)


def remote(src, dst, ssem, rsem, to):
    return pltpu.make_async_remote_copy(
        src_ref=src, dst_ref=dst, send_sem=ssem, recv_sem=rsem, device_id=to, device_id_type=MESH
    )


def greet(peers):
    barrier = pltpu.get_barrier_semaphore()
    for peer in peers:
        pl.semaphore_signal(barrier, inc=1, device_id=peer, device_id_type=MESH)
    pl.semaphore_wait(barrier, len(peers))


def grads_kernel(
    act, og, g_out, fin_out, fout_out,
    abuf, gbuf, pbuf, h1, h2, sbuf, xr, fs, fbuf, frecv, obuf, orecv,
    aloc, ad2d_s, ad2d_r, gloc, gs, gr, ys, yr, ws, wr, h1s, h1r, h2s, h2r, xs, xrs, fss, frs, oss, ors,
):
    xh, xl, y, z, c = where()
    me = xh * 8 + z * 2 + c
    mate = device(xh, xl, y, z, 1 - c)
    up, down = device(xh, xl, y + 1, z, c), device(xh, xl, y + 3, z, c)
    fore, back = device(xh, xl, y, z + 1, c), device(xh, xl, y, z + 3, c)
    beside = device(xh, 1 - xl, y, z, c)
    peers = [((me + s) % 16, xl * 4 + y) for s in range(1, 16)]
    peers += [up, down, beside, device(1 - xh, 1 - xl, y, z, c)]
    greet(peers)

    mine = pl.ds(pl.multiple_of(c * TOK, TOK), TOK)
    own_cols = pl.ds(pl.multiple_of(xl * ROWS, ROWS), ROWS)
    other_cols = pl.ds(pl.multiple_of((1 - xl) * ROWS, ROWS), ROWS)

    def cols(p):
        return pl.ds(pl.multiple_of(p * PW, PW), PW)

    def local_a(p):
        return pltpu.make_async_copy(
            act.at[:, pl.ds(pl.multiple_of(c * BLK + p * PW, PW), PW)], abuf.at[0, mine, cols(p)], aloc.at[p])

    def mate_a(p):
        return remote(
            act.at[:, pl.ds(pl.multiple_of((1 - c) * BLK + p * PW, PW), PW)], abuf.at[0, mine, cols(p)],
            ad2d_s.at[p], ad2d_r.at[p], mate)

    for p in range(NP):
        mate_a(p).start()
        local_a(p).start()
    g_local = pltpu.make_async_copy(og, gbuf.at[mine, own_cols], gloc)
    g_beside = remote(og, gbuf.at[mine, own_cols], gs.at[0], gr.at[0], beside)
    g_mate = remote(og, gbuf.at[mine, own_cols], gs.at[1], gr.at[1], mate)
    g_pass = remote(gbuf.at[mine, other_cols], gbuf.at[mine, other_cols], gs.at[2], gr.at[2], mate)
    g_local.start()
    g_beside.start()
    g_mate.start()

    def send_up(p):
        return remote(abuf.at[0, :, cols(p)], abuf.at[3, :, cols(p)], ys.at[0, p], yr.at[0, p], up)

    def send_down(p):
        return remote(abuf.at[0, :, cols(p)], abuf.at[1, :, cols(p)], ys.at[1, p], yr.at[1, p], down)

    def pass_down(p):
        return remote(
            abuf.at[1, 0:TOK, cols(p)], abuf.at[2, 0:TOK, cols(p)], ws.at[0, p], wr.at[0, p], down)

    def pass_up(p):
        return remote(
            abuf.at[3, TOK : 2 * TOK, cols(p)], abuf.at[2, TOK : 2 * TOK, cols(p)], ws.at[1, p], wr.at[1, p], up)

    def ready(p):
        local_a(p).wait()
        mate_a(p).wait_recv()

    for p in range(NP):
        ready(p)
        if p < 2:
            send_up(p).start()
            send_down(p).start()

    def factor_rows(p, carry):
        fs[cols(p), :] = contract0(abuf[0, :, cols(p)], abuf[0])
        return carry

    lax.fori_loop(0, NP, factor_rows, 0)
    fbuf[:, 48:64, :] = jnp.zeros((16, 16, BLK), bf16)

    def strips(r, carry):
        fbuf[r, 0:56, :] = fs[pl.ds(pl.multiple_of(r * 56, 8), 56), :].astype(bf16)
        return carry

    lax.fori_loop(0, 16, strips, 0)
    g_local.wait()
    g_here = gbuf[mine, own_cols]
    obuf[...] = contract0(g_here, g_here).astype(bf16)

    def send_factor(s):
        r = (me + s) % 16
        return (
            remote(fbuf.at[r], frecv.at[s], fss.at[s], frs.at[s], (r, xl * 4 + y)),
            remote(obuf.at[pl.ds(pl.multiple_of(r * 32, 32), 32), :], orecv.at[s], oss.at[s], ors.at[s],
                   (r, xl * 4 + y)),
        )

    def start_factor(s, carry):
        for copy in send_factor(s):
            copy.start()
        return carry

    lax.fori_loop(1, 16, start_factor, 0)
    g_beside.wait_recv()
    g_pass.start()
    g_mate.wait_recv()
    g_pass.wait_recv()

    def partial(d, p):
        e = (y - z + d + 4) % 4
        a = abuf[d, :, cols(p)]
        for tx in range(2):
            pbuf[e, tx, cols(p), :] = contract0(a, gbuf[:, tx * ROWS : (tx + 1) * ROWS]).astype(bf16)

    def hop1(p):
        return (
            remote(pbuf.at[2, 0, cols(p), :], h1.at[0, cols(p), :], h1s.at[0, p], h1r.at[0, p], fore),
            remote(pbuf.at[2, 1, cols(p), :], h1.at[1, cols(p), :], h1s.at[1, p], h1r.at[1, p], back),
        )

    def hop2(p):
        return (
            remote(pbuf.at[1, :, cols(p), :], h2.at[0, :, cols(p), :], h2s.at[0, p], h2r.at[0, p], fore),
            remote(pbuf.at[3, :, cols(p), :], h2.at[1, :, cols(p), :], h2s.at[1, p], h2r.at[1, p], back),
        )

    def to_owner(tx, p):
        return remote(
            sbuf.at[tx, cols(p), :], xr.at[xh, cols(p), :], xs.at[tx, p], xrs.at[xh, p], device(xl, tx, y, z, c))

    def from_half(kx, p):
        return remote(
            sbuf.at[0, cols(p), :], xr.at[kx, cols(p), :], xs.at[0, p], xrs.at[kx, p], beside)

    def is_self(tx):
        return jnp.logical_and(xh == xl, xl == tx)

    def comes_from_self(kx):
        return jnp.logical_and(xh == xl, kx == xh)

    def step(i, carry):
        @pl.when(jnp.logical_and(i >= 2, i < NP + 2))
        def _():
            p = i - 2
            for copy in hop1(p):
                copy.wait_recv()
            pbuf[1, 0, cols(p), :] = (
                pbuf[1, 0, cols(p), :].astype(f32) + h1[0, cols(p), :].astype(f32)).astype(bf16)
            pbuf[3, 1, cols(p), :] = (
                pbuf[3, 1, cols(p), :].astype(f32) + h1[1, cols(p), :].astype(f32)).astype(bf16)
            for copy in hop2(p):
                copy.start()

        @pl.when(i < NP)
        def _():
            @pl.when(i + 2 < NP)
            def _():
                send_up(i).wait_send()
                send_down(i).wait_send()
                send_up(i + 2).start()
                send_down(i + 2).start()

            partial(0, i)
            send_down(i).wait_recv()
            pass_down(i).start()
            send_up(i).wait_recv()
            pass_up(i).start()
            partial(1, i)
            partial(3, i)

        @pl.when(jnp.logical_and(i >= 1, i < NP + 1))
        def _():
            p = i - 1
            pass_down(p).wait_recv()
            pass_up(p).wait_recv()
            partial(2, p)
            for copy in hop1(p):
                copy.start()

        @pl.when(jnp.logical_and(i >= 3, i < NP + 3))
        def _():
            p = i - 3
            for copy in hop2(p):
                copy.wait_recv()
            for tx in range(2):
                total = (pbuf[0, tx, cols(p), :].astype(f32) + h2[0, tx, cols(p), :].astype(f32)
                         + h2[1, tx, cols(p), :].astype(f32))
                sbuf[tx, cols(p), :] = total.astype(bf16)

                @pl.when(is_self(tx))
                def _():
                    xr[xh, cols(p), :] = total.astype(bf16)

                @pl.when(jnp.logical_not(is_self(tx)))
                def _():
                    to_owner(tx, p).start()

        @pl.when(i >= 4)
        def _():
            p = i - 4
            for kx in range(2):
                @pl.when(jnp.logical_not(comes_from_self(kx)))
                def _():
                    from_half(kx, p).wait_recv()
            g_out[cols(p), :] = (xr[0, cols(p), :].astype(f32) + xr[1, cols(p), :].astype(f32)) * SCALE

        return carry

    lax.fori_loop(0, NP + 4, step, 0)

    def take(s, carry):
        for copy in send_factor(s):
            copy.wait_recv()
        return carry

    lax.fori_loop(1, 16, take, 0)
    here = fbuf[me, 0:56, :].astype(f32)
    there = frecv[1, 0:56, :].astype(f32)
    for s in range(2, 16):
        term = frecv[s, 0:56, :].astype(f32)
        if s % 2 == 0:
            here += term
        else:
            there += term
    fin_out[c] = here * SCALE
    fin_out[1 - c] = there * SCALE
    total = obuf[pl.ds(pl.multiple_of(me * 32, 32), 32), :].astype(f32)
    for s in range(1, 16):
        total += orecv[s].astype(f32)
    fout_out[...] = total * SCALE

    for copy in (g_beside, g_mate, g_pass):
        copy.wait_send()

    def finish(p, carry):
        mate_a(p).wait_send()
        for copy in (pass_down(p), pass_up(p)) + hop1(p) + hop2(p):
            copy.wait_send()
        for tx in range(2):
            @pl.when(jnp.logical_not(is_self(tx)))
            def _():
                to_owner(tx, p).wait_send()
        return carry

    lax.fori_loop(0, NP, finish, 0)
    for p in range(NP - 2, NP):
        send_up(p).wait_send()
        send_down(p).wait_send()

    def finish_factor(s, carry):
        for copy in send_factor(s):
            copy.wait_send()
        return carry

    lax.fori_loop(1, 16, finish_factor, 0)


def weight_grads(activations, output_grads):
    dma = pltpu.SemaphoreType.DMA
    any_spec = pl.BlockSpec(memory_space=pl.ANY)
    vmem = pl.BlockSpec(memory_space=pltpu.VMEM)
    return pl.pallas_call(
        grads_kernel,
        out_shape=(
            jax.ShapeDtypeStruct((BLK, ROWS), f32),
            jax.ShapeDtypeStruct((2, 56, BLK), f32),
            jax.ShapeDtypeStruct((32, ROWS), f32),
        ),
        in_specs=[any_spec, any_spec],
        out_specs=(vmem, vmem, vmem),
        scratch_shapes=[
            pltpu.VMEM((4, 2 * TOK, BLK), bf16),
            pltpu.VMEM((2 * TOK, 2 * ROWS), bf16),
            pltpu.VMEM((4, 2, BLK, ROWS), bf16),
            pltpu.VMEM((2, BLK, ROWS), bf16),
            pltpu.VMEM((2, 2, BLK, ROWS), bf16),
            pltpu.VMEM((2, BLK, ROWS), bf16),
            pltpu.VMEM((2, BLK, ROWS), bf16),
            pltpu.VMEM((BLK, BLK), f32),
            pltpu.VMEM((16, 64, BLK), bf16),
            pltpu.VMEM((16, 64, BLK), bf16),
            pltpu.VMEM((ROWS, ROWS), bf16),
            pltpu.VMEM((16, 32, ROWS), bf16),
            dma((NP,)), dma((NP,)), dma((NP,)),
            dma, dma((3,)), dma((3,)),
            dma((2, NP)), dma((2, NP)), dma((2, NP)), dma((2, NP)),
            dma((2, NP)), dma((2, NP)), dma((2, NP)), dma((2, NP)),
            dma((2, NP)), dma((2, NP)),
            dma((16,)), dma((16,)), dma((16,)), dma((16,)),
        ],
        compiler_params=pltpu.CompilerParams(
            collective_id=0, has_side_effects=True, vmem_limit_bytes=52 * 2**20),
        cost_estimate=pl.CostEstimate(flops=9_500_000_000, bytes_accessed=6_000_000, transcendentals=0),
        name="weight_grads",
    )(activations, output_grads)


def body(activations, output_grads, basis_in, eigen_in, basis_out, eigen_out):
    highest = lax.Precision.HIGHEST
    grad, fin, factor_out = weight_grads(activations, output_grads)
    factor_in = jnp.transpose(fin, (1, 0, 2))
    grad = grad[None]
    values_in = eigen_in.reshape(1, BLK)
    rotated = jnp.einsum("bij,bik->bjk", basis_in, grad, precision=highest)
    rotated = jnp.einsum("bjk,kl->bjl", rotated, basis_out, precision=highest)
    scaled = rotated / (values_in[:, :, None] * eigen_out[None, None, :] + damping)
    back = jnp.einsum("bjl,bij->bil", scaled, basis_in, precision=highest)
    back = jnp.einsum("bil,kl->bik", back, basis_out, precision=highest)
    worker_slab = back.reshape(BLK, ROWS).astype(jnp.bfloat16)
    update = lax.all_gather(worker_slab, "dp", axis=0, tiled=True)
    return (update, factor_in, factor_out)


def solution(mesh):
    in_specs = (
        P("dp", "tensor"),
        P("dp", "tensor"),
        P("dp", None, None),
        P("dp"),
        P("tensor", None),
        P("tensor"),
    )
    out_specs = (P(None, "tensor"), P("dp", "tensor", None), P("dp", "tensor"))
    return jax.shard_map(body, mesh=mesh, in_specs=in_specs, out_specs=out_specs, check_vma=False)
```

time: 651 us -> 290 us (0.45)
  waiting for transfers between devices: 559 us -> 101 us
  Pallas kernels: 0 us -> 126 us
  matrix products: 49.6 us -> 31.1 us
  local copies, waits for them, and re-layouts: 24.1 us -> 16.9 us
    all_gather x1 -> x0, waiting for transfers between devices: 156 us -> none  [body(): whole = lax.all_gather(activations, 'tensor', axis=1, tiled=True)]
    unnamed x6 -> x1, waiting for transfers between devices: 150 us -> 0.02 us
    reduce_scatter x2 -> x0, waiting for transfers between devices: 150 us -> none  [body(): lax.psum_scatter((contract_rows(part, output_grads) / total_tokens).astyp...]
    pallas_call x0 -> x1, Pallas kernels: none -> 126 us  [weight_grads(): pl.pallas_call(grads_kernel, out_shape=(jax.ShapeDtypeStruct((BLK, ROWS),...]
    dot_general x4 -> x1, matrix products: 27.3 us -> 8.65 us  [body(): rotated = jnp.einsum('bij,bik->bjk', basis_in, grad, precision=highest)]
    convert_element_type x1 -> x0, local copies, waits for them, and re-layouts: 10.4 us -> none  [reduce_input_factor(): return lax.psum_scatter((jnp.einsum('tbi,tbj->ibj', local_blocks, local_b...]
    unnamed x12 -> x15, local copies, waits for them, and re-layouts: 13.7 us -> 16.9 us
  transfers between devices with their start and end apart: 5 -> 1, of which waited for: 5 -> 1; matrix products, arithmetic and copies ran while one was open for 8% -> 1% of each run, Pallas kernels for 0% -> 0%
where the time goes in v1:
time: 290 us
  Pallas kernels  126 us (43%)
  waiting for transfers between devices  101 us (35%)
  matrix products  31.1 us (11%)
  local copies, waits for them, and re-layouts  16.9 us (6%)
  between operations  14.1 us (5%)
    pallas_call x1, Pallas kernels, weight_grads(): pl.pallas_call(grads_kernel, out_shape=(jax.ShapeDtypeStruct((BLK, ROWS),...  126 us
    all_gather x1, waiting for transfers between devices, body(): update = lax.all_gather(worker_slab, 'dp', axis=0, tiled=True)  101 us
    unnamed x15, local copies, waits for them, and re-layouts  16.9 us
    dot_general x1, matrix products, body(): back = jnp.einsum('bjl,bij->bil', scaled, basis_in, precision=highest)  12.2 us
    dot_general x1, matrix products, body(): rotated = jnp.einsum('bij,bik->bjk', basis_in, grad, precision=highest)  8.65 us
    dot_general x1, matrix products, body(): back = jnp.einsum('bil,kl->bik', back, basis_out, precision=highest)  7.21 us
  transfers between devices with their start and end apart: 1, of which 1 were waited for; matrix products, arithmetic and copies ran while one was open for 1% of the time, Pallas kernels for 0%

profile of v1, /device:TPU:1, one launch (start us, length us, event | category | flops | bytes accessed | tf_op | source)
XLA Modules:
  0.0 289.8 jit_solution(5646886606233657219)
XLA Ops:
  7.2 0.0 copy-start
  7.2 0.0 all-gather.2.cloned.1.call-start
  7.2 0.0 copy-start.2
  7.2 1.2 copy-done.2
  8.4 126.3 %weight_grads.1 = (f32[896,512]{1,0:T(8,128)}, f32[2,56,896]{2,1,0:T(8,128)S(1)}, f32[32,512]{1,0:T(8,128)S(1)}) custom-call(bf16[512,1792]{1,0:T(8,128)(2,1)} %act.1, bf16[512,512]{1,0:T(8,128)(2,1)S(1)} %copy-done.2), custom_call_target="tpu_custom_call" | custom-call | flops 9500000256 | bytes 6000000 | tf_op jit(solution)/shard_map/weight_grads/pallas_call | solution.py:300
  134.8 0.0 copy-start.1
  134.8 0.0 copy-done
  134.8 0.0 copy-start.3
  134.8 8.7 %fusion.2 = f32[512,896]{1,0:T(8,128)S(1)} fusion(f32[896,512]{1,0:T(8,128)} %get-tuple-element.6, f32[1,896,896]{2,1,0:T(8,128)S(1)} %copy-done), kind=kOutput, calls=%fused_computation.2 | convolution fusion | flops 4932501504 | bytes 6881280 | tf_op jit(solution)/shard_map/bij,bik->bjk/dot_general | solution.py:342
  143.5 0.0 copy-done.1
  143.5 0.0 copy-done.3
  143.5 0.0 copy-start.4
  143.5 0.0 copy-start.5
  143.5 3.1 %fusion.11 = f32[896,512]{1,0:T(8,128)S(1)} fusion(f32[512,896]{1,0:T(8,128)S(1)} %fusion.2, f32[512,512]{1,0:T(8,128)S(1)} %copy-done.3), kind=kOutput, calls=%fused_computation.12 | convolution fusion | flops 2818572288 | bytes 4718592 | tf_op jit(solution)/shard_map/bjk,kl->bjl/dot_general | solution.py:343
  146.6 0.0 copy-done.4
  146.6 0.0 copy-done.5
  146.6 12.2 %fusion = f32[512,896]{1,0:T(8,128)S(1)} fusion(f32[1,896,896]{2,1,0:T(8,128)S(1)} %copy-done, f32[896,512]{1,0:T(8,128)S(1)} %fusion.11, f32[512]{0:T(512)S(1)} %copy-done.5, f32[896]{0:T(1024)S(1)} %copy-done.4), kind=kOutput, calls=%fused_computation | convolution fusion | flops 4933877760 | bytes 6886912 | tf_op jit(solution)/shard_map/bjl,bij->bil/dot_general | solution.py:345
  158.8 7.2 %convolution_convert_fusion = bf16[896,512]{1,0:T(8,128)(2,1)} fusion(f32[512,896]{1,0:T(8,128)S(1)} %fusion, f32[512,512]{1,0:T(8,128)S(1)} %copy-done.3), kind=kOutput, calls=%fused_computation.7 | convolution fusion | flops 2819031040 | bytes 3801088 | tf_op jit(solution)/shard_map/bil,kl->bik/dot_general | solution.py:346
  166.0 0.0 all-gather.2.cloned.1.call-update
  166.0 2.0 copy.9
  168.0 101.2 %all-gather.2.cloned.1.call-done = bf16[14336,512]{1,0:T(8,128)(2,1)} async-done(((bf16[896,512]{1,0:T(8,128)(2,1)}), bf16[14336,512]{1,0:T(8,128)(2,1)}) %all-gather.2.cloned.1.call-update) | async-done | bytes 14680080 | tf_op jit(solution)/shard_map/all_gather | solution.py:348
  269.2 13.1 %copy.12 = bf16[14336,512]{1,0:T(8,128)(2,1)} copy(bf16[14336,512]{1,0:T(8,128)(2,1)} %all-gather.2.cloned.1.call-done) | data formatting | bytes 29360128
  282.3 0.6 copy.13
Async XLA Ops:
  7.2 127.6 %copy-start = (f32[1,896,896]{2,1,0:T(8,128)S(1)}, f32[1,896,896]{2,1,0:T(8,128)}, u32[]{:S(2)}) copy-start(f32[1,896,896]{2,1,0:T(8,128)} %param.8) | copy-start | bytes 9633796
  7.2 262.0 %all-gather.2.cloned.1.call-start = ((), (), s32[]{:S(2)}) async-start(), calls=%async_computation | async-start | bytes 15597568 | tf_op jit(solution)/shard_map/all_gather | solution.py:348
  7.2 1.2 copy-start.2
  134.8 8.7 %copy-start.1 = (f32[2,56,896]{2,1,0:T(8,128)}, f32[2,56,896]{2,1,0:T(8,128)S(1)}, u32[]{:S(2)}) copy-start(f32[2,56,896]{2,1,0:T(8,128)S(1)} %get-tuple-element.7) | copy-start | bytes 1204228
  134.8 8.7 %copy-start.3 = (f32[512,512]{1,0:T(8,128)S(1)}, f32[512,512]{1,0:T(8,128)}, u32[]{:S(2)}) copy-start(f32[512,512]{1,0:T(8,128)} %param.10) | copy-start | bytes 3145732
  143.5 3.1 %copy-start.4 = (f32[896]{0:T(1024)S(1)}, f32[896]{0:T(1024)}, u32[]{:S(2)}) copy-start(f32[896]{0:T(1024)} %param.9) | copy-start | bytes 10756
  143.5 3.1 %copy-start.5 = (f32[512]{0:T(512)S(1)}, f32[512]{0:T(512)}, u32[]{:S(2)}) copy-start(f32[512]{0:T(512)} %param.11) | copy-start | bytes 6148
Sparse Core Ops, SparseCore 0:
  166.2 103.0 all-gather.1

commit v2 on v1

--- a/solution.py
+++ b/solution.py
@@ -333,19 +333,177 @@
     )(activations, output_grads)
 
 
+def split(x):
+    high = x.astype(bf16)
+    return high, (x - high.astype(f32)).astype(bf16)
+
+
+def dot(a, b):
+    return jnp.dot(a, b, preferred_element_type=f32)
+
+
+PARTS = ((0, 256), (256, 256), (512, 192), (704, 192))
+FIRST = (0, 512)
+LAST = (512, 384)
+
+
+def update_kernel(
+    g, basis_in, eigen_in, basis_out, eigen_out, u,
+    qh, ql, vbuf,
+    zs, zr, fs, fr, xs, xr, ds, dr,
+):
+    xh, xl, y, z, c = where()
+    me = xh * 8 + z * 2 + c
+    mate = device(xh, xl, y, z, 1 - c)
+    fore, back = device(xh, xl, y, z + 1, c), device(xh, xl, y, z + 3, c)
+    across = device(1 - xh, xl, y, z, c)
+    greet([mate, fore, back, across])
+
+    for p in range(NP):
+        high, low = split(basis_in[0, p * PW : (p + 1) * PW, :])
+        qh[p * PW : (p + 1) * PW, :] = high
+        ql[p * PW : (p + 1) * PW, :] = low
+    gh, gl = split(g[...])
+    oh, ol = split(basis_out[...])
+    for start, size in (FIRST, LAST):
+        rows = slice(start, start + size)
+        mid = contract0(qh[:, rows], gh) + contract0(qh[:, rows], gl) + contract0(ql[:, rows], gh)
+        mh, ml = split(mid)
+        turned = dot(mh, oh) + dot(mh, ol) + dot(ml, oh)
+        column = jnp.transpose(jnp.broadcast_to(eigen_in[:, rows], (128, size)))
+        for k in range(ROWS // 128):
+            lanes = slice(k * 128, (k + 1) * 128)
+            scaled = turned[:, lanes] / (column * eigen_out[:, lanes] + damping)
+            vbuf[rows, lanes] = scaled.astype(bf16)
+        back_out = lax.dot_general(
+            vbuf[rows, :], oh, (((1,), (1,)), ((), ())), preferred_element_type=f32)
+        vbuf[rows, :] = back_out.astype(bf16)
+
+    def part(other, dz, core, start, size):
+        half = (1 - xh) if other else xh
+        base = (half * 8 + ((z + dz) % 4) * 2 + core) * BLK
+        return u.at[pl.ds(pl.multiple_of(base + start, 64), size), :]
+
+    def copy(other, dz, start, size, ssem, rsem, to):
+        return remote(part(other, dz, c, start, size), part(other, dz, c, start, size), ssem, rsem, to)
+
+    waits = []
+
+    def go(descriptor):
+        descriptor.start()
+        waits.append(descriptor)
+        return descriptor
+
+    def ring(sem, other, start, size):
+        go(copy(other, 0, start, size, zs.at[0, sem], zr.at[0, sem], fore))
+        go(copy(other, 0, start, size, zs.at[1, sem], zr.at[1, sem], back))
+
+    def ring_take(sem, other, start, size):
+        copy(other, 3, start, size, zs.at[0, sem], zr.at[0, sem], fore).wait_recv()
+        copy(other, 1, start, size, zs.at[1, sem], zr.at[1, sem], back).wait_recv()
+
+    def relay(sem, other, start, size):
+        half = size // 2
+        go(copy(other, 3, start, half, fs.at[0, sem], fr.at[0, sem], fore))
+        go(copy(other, 1, start + half, half, fs.at[1, sem], fr.at[1, sem], back))
+
+    def relay_take(sem, other, start, size):
+        half = size // 2
+        copy(other, 2, start, half, fs.at[0, sem], fr.at[0, sem], fore).wait_recv()
+        copy(other, 2, start + half, half, fs.at[1, sem], fr.at[1, sem], back).wait_recv()
+
+    def cross(sem, dz, start, size):
+        go(copy(False, dz, start, size, xs.at[sem], xr.at[sem], across))
+
+    def cross_take(sem, dz, start, size):
+        copy(True, dz, start, size, xs.at[sem], xr.at[sem], across).wait_recv()
+
+    given = []
+
+    def share(other, dz, start, size):
+        sem = len(given)
+        go(copy(other, dz, start, size, ds.at[sem], dr.at[sem], mate))
+        given.append((other, dz, start, size))
+
+    for k, (start, size) in enumerate(PARTS):
+        block = dot(qh[start : start + size, :], vbuf[...]).astype(bf16)
+        u[pl.ds(pl.multiple_of(me * BLK + start, 64), size), :] = block
+        if k < 2:
+            cross(k, 0, start, size)
+            ring(k, False, start, size)
+        if k == 3:
+            ring(2, False, *LAST)
+            cross(2, 0, *LAST)
+    share(False, 0, *FIRST)
+    share(False, 0, *LAST)
+    for k in range(2):
+        ring_take(k, False, *PARTS[k])
+        relay(k, False, *PARTS[k])
+    for k in range(2):
+        cross_take(k, 0, *PARTS[k])
+        ring(3 + k, True, *PARTS[k])
+    ring_take(2, False, *LAST)
+    relay(2, False, *LAST)
+    cross(3, 1, *LAST)
+    cross(4, 3, *LAST)
+    for dz in (1, 3):
+        share(False, dz, 0, BLK)
+    share(True, 0, *FIRST)
+    for k in range(2):
+        relay_take(k, False, *PARTS[k])
+    share(False, 2, *FIRST)
+    relay_take(2, False, *LAST)
+    cross(5, 2, *LAST)
+    share(False, 2, *LAST)
+    cross_take(2, 0, *LAST)
+    share(True, 0, *LAST)
+    for k in range(2):
+        ring_take(3 + k, True, *PARTS[k])
+        relay(3 + k, True, *PARTS[k])
+    share(True, 1, *FIRST)
+    share(True, 3, *FIRST)
+    cross_take(3, 1, *LAST)
+    share(True, 1, *LAST)
+    cross_take(4, 3, *LAST)
+    share(True, 3, *LAST)
+    cross_take(5, 2, *LAST)
+    share(True, 2, *LAST)
+    for k in range(2):
+        relay_take(3 + k, True, *PARTS[k])
+        share(True, 2, *PARTS[k])
+    for sem, (other, dz, start, size) in enumerate(given):
+        ref = part(other, dz, 1 - c, start, size)
+        remote(ref, ref, ds.at[sem], dr.at[sem], mate).wait_recv()
+    for descriptor in waits:
+        descriptor.wait_send()
+
+
+def rotate_and_gather(grad, basis_in, eigen_in, basis_out, eigen_out):
+    dma = pltpu.SemaphoreType.DMA
+    vmem = pl.BlockSpec(memory_space=pltpu.VMEM)
+    return pl.pallas_call(
+        update_kernel,
+        out_shape=pltpu.VMEM((16 * BLK, ROWS), bf16),
+        in_specs=[vmem] * 5,
+        out_specs=vmem,
+        scratch_shapes=[
+            pltpu.VMEM((BLK, BLK), bf16),
+            pltpu.VMEM((BLK, BLK), bf16),
+            pltpu.VMEM((BLK, ROWS), bf16),
+            dma((2, 5)), dma((2, 5)), dma((2, 5)), dma((2, 5)),
+            dma((6,)), dma((6,)), dma((20,)), dma((20,)),
+        ],
+        compiler_params=pltpu.CompilerParams(
+            collective_id=1, has_side_effects=True, vmem_limit_bytes=36 * 2**20),
+        cost_estimate=pl.CostEstimate(flops=5_000_000_000, bytes_accessed=20_000_000, transcendentals=0),
+        name="rotate_and_gather",
+    )(grad, basis_in, eigen_in, basis_out, eigen_out)
+
+
 def body(activations, output_grads, basis_in, eigen_in, basis_out, eigen_out):
-    highest = lax.Precision.HIGHEST
     grad, fin, factor_out = weight_grads(activations, output_grads)
     factor_in = jnp.transpose(fin, (1, 0, 2))
-    grad = grad[None]
-    values_in = eigen_in.reshape(1, BLK)
-    rotated = jnp.einsum("bij,bik->bjk", basis_in, grad, precision=highest)
-    rotated = jnp.einsum("bjk,kl->bjl", rotated, basis_out, precision=highest)
-    scaled = rotated / (values_in[:, :, None] * eigen_out[None, None, :] + damping)
-    back = jnp.einsum("bjl,bij->bil", scaled, basis_in, precision=highest)
-    back = jnp.einsum("bil,kl->bik", back, basis_out, precision=highest)
-    worker_slab = back.reshape(BLK, ROWS).astype(jnp.bfloat16)
-    update = lax.all_gather(worker_slab, "dp", axis=0, tiled=True)
+    update = rotate_and_gather(grad, basis_in, eigen_in.reshape(1, BLK), basis_out, eigen_out.reshape(1, ROWS))
     return (update, factor_in, factor_out)
 
 

time: 290 us -> 205 us (0.71)
  waiting for transfers between devices: 101 us -> 0 us
  Pallas kernels: 126 us -> 191 us
  matrix products: 31.1 us -> 0 us
  between operations: 14.1 us -> 0.65 us
  local copies, waits for them, and re-layouts: 16.9 us -> 10.3 us
    all_gather x1 -> x0, waiting for transfers between devices: 101 us -> none  [body(): update = lax.all_gather(worker_slab, 'dp', axis=0, tiled=True)]
    pallas_call x0 -> x1, Pallas kernels: none -> 65 us  [rotate_and_gather(): pl.pallas_call(update_kernel, out_shape=pltpu.VMEM((16 * BLK, ROWS), bf16...]
    dot_general x4 -> x0, matrix products: 31.1 us -> none  [the longest x1 12.2 us: body(): back = jnp.einsum('bjl,bij->bil', scaled, basis_in, precision=highest)]
    unnamed x15 -> x11, local copies, waits for them, and re-layouts: 16.9 us -> 9.6 us
  transfers between devices with their start and end apart: 1 -> 0, of which waited for: 1 -> 0; matrix products, arithmetic and copies ran while one was open for 1% -> 0% of each run, Pallas kernels for 0% -> 0%
where the time goes in v2:
time: 205 us; the launch traced here: 202 us
  Pallas kernels  191 us (93%)
  local copies, waits for them, and re-layouts  10.3 us (5%)
    pallas_call x1, Pallas kernels, weight_grads(): pl.pallas_call(grads_kernel, out_shape=(jax.ShapeDtypeStruct((BLK, ROWS),...  126 us
    pallas_call x1, Pallas kernels, rotate_and_gather(): pl.pallas_call(update_kernel, out_shape=pltpu.VMEM((16 * BLK, ROWS), bf16...  65 us
    unnamed x11, local copies, waits for them, and re-layouts  9.6 us

profile of v2, /device:TPU:1, one launch (start us, length us, event | category | flops | bytes accessed | tf_op | source)
XLA Modules:
  0.0 202.0 jit_solution(14761245406499770705)
XLA Ops:
  0.6 0.7 reshape.12.eigen_in
  1.3 0.0 copy-start.3
  1.3 1.0 copy-done.3
  2.4 0.0 copy-start.1
  2.4 0.0 copy-start.2
  2.4 126.1 %weight_grads.1 = (f32[896,512]{1,0:T(8,128)}, f32[2,56,896]{2,1,0:T(8,128)S(1)}, f32[32,512]{1,0:T(8,128)S(1)}) custom-call(bf16[512,1792]{1,0:T(8,128)(2,1)} %act.1, bf16[512,512]{1,0:T(8,128)(2,1)S(1)} %copy-done.3), custom_call_target="tpu_custom_call" | custom-call | flops 9500000256 | bytes 6000000 | tf_op jit(solution)/shard_map/weight_grads/pallas_call | solution.py:300
  128.5 1.0 copy.9
  129.5 0.0 copy-done.1
  129.5 0.0 copy-done.2
  129.5 0.0 copy-start
  129.5 1.5 copy-done
  131.0 65.0 %rotate_and_gather.1 = bf16[14336,512]{1,0:T(8,128)(2,1)S(1)} custom-call(f32[896,512]{1,0:T(8,128)S(1)} %copy-done, f32[1,896,896]{2,1,0:T(8,128)} %basis_in.1, f32[1,896]{1,0:T(1,128)S(1)} %reshape.12.eigen_in, f32[512,512]{1,0:T(8,128)S(1)} %copy-done.1, f32[1,512]{1,0:T(1,128)S(1)} %bitcast.3), custom_call_target="tpu_custom_call" | custom-call | flops 5000000000 | bytes 20000000 | tf_op jit(solution)/shard_map/rotate_and_gather/pallas_call | solution.py:484
  195.9 5.5 %copy.12 = bf16[14336,512]{1,0:T(8,128)(2,1)} copy(bf16[14336,512]{1,0:T(8,128)(2,1)S(1)} %rotate_and_gather.1) | data formatting | bytes 29360128
  201.4 0.6 copy.13
Async XLA Ops:
  1.3 1.0 copy-start.3
  2.4 127.1 %copy-start.1 = (f32[512,512]{1,0:T(8,128)S(1)}, f32[512,512]{1,0:T(8,128)}, u32[]{:S(2)}) copy-start(f32[512,512]{1,0:T(8,128)} %basis_out.1) | copy-start | bytes 3145732
  2.4 127.1 %copy-start.2 = (f32[512]{0:T(512)S(1)}, f32[512]{0:T(512)}, u32[]{:S(2)}) copy-start(f32[512]{0:T(512)} %param.11) | copy-start | bytes 6148
  129.5 1.5 copy-start

commit v3 on v1

v3 whole, which is shorter than its diff:
```python
import functools
import jax
import jax.numpy as jnp
from jax import lax
from jax.experimental import pallas as pl
from jax.experimental.pallas import tpu as pltpu
from jax.sharding import PartitionSpec as P

MESH = pl.DeviceIdType.MESH
BLK = 896
ROWS = 512
TOK = 512
NP = 7
PW = 128
SCALE = 1.0 / 8192
LAG2, LAG3, LAG4 = 2, 3, 4
STRIPS = NP + 1
damping = 0.01
f32, bf16 = jnp.float32, jnp.bfloat16


def where():
    dp, t = lax.axis_index("dp"), lax.axis_index("tensor")
    return dp // 8, t // 4, t % 4, (dp // 2) % 4, dp % 2


def device(xh, xl, y, z, c):
    return (xh * 8 + (z % 4) * 2 + c, xl * 4 + (y % 4))


def contract0(a, b):
    return lax.dot_general(a, b, (((0,), (0,)), ((), ())), preferred_element_type=f32)


def remote(src, dst, ssem, rsem, to):
    return pltpu.make_async_remote_copy(
        src_ref=src, dst_ref=dst, send_sem=ssem, recv_sem=rsem, device_id=to, device_id_type=MESH
    )


def greet(peers):
    barrier = pltpu.get_barrier_semaphore()
    for peer in peers:
        pl.semaphore_signal(barrier, inc=1, device_id=peer, device_id_type=MESH)
    pl.semaphore_wait(barrier, len(peers))


def split(x):
    high = x.astype(bf16)
    return high, (x - high.astype(f32)).astype(bf16)


def dot(a, b):
    return jnp.dot(a, b, preferred_element_type=f32)


PARTS = ((0, 256), (256, 256), (512, 192), (704, 192))
FIRST = (0, 512)
LAST = (512, 384)


def step_kernel(
    act, og, basis_in, eigen_in, basis_out, eigen_out, u, fin_out, fout_out,
    abuf, gbuf, pbuf, h1, h2, sbuf, xr, fs, fbuf, fswap, frecv, obuf, oswap, orecv,
    aloc, ad2d_s, ad2d_r, gloc, gs, gr, ys, yr, ws, wr, h1s, h1r, h2s, h2r, xs, xrs, fss, frs, oss, ors,
    qh, ql, r1, vbuf, qloc, zs, zr, vs, vr, cs, cr, ds, dr,
):
    xh, xl, y, z, c = where()
    me = xh * 8 + z * 2 + c
    mate = device(xh, xl, y, z, 1 - c)
    up, down = device(xh, xl, y + 1, z, c), device(xh, xl, y + 3, z, c)
    fore, back = device(xh, xl, y, z + 1, c), device(xh, xl, y, z + 3, c)
    beside = device(xh, 1 - xl, y, z, c)
    across = device(1 - xh, xl, y, z, c)
    column = [(dz, cc) for cc in range(2) for dz in range(4)][1:]
    peers = [device(xh, xl, y, z + dz, (c + cc) % 2) for dz, cc in column]
    greet(peers + [up, down, beside, across, device(1 - xh, 1 - xl, y, z, c)])

    mine = pl.ds(pl.multiple_of(c * TOK, TOK), TOK)
    own_cols = pl.ds(pl.multiple_of(xl * ROWS, ROWS), ROWS)
    other_cols = pl.ds(pl.multiple_of((1 - xl) * ROWS, ROWS), ROWS)

    def cols(p):
        return pl.ds(pl.multiple_of(p * PW, PW), PW)

    def local_a(p):
        return pltpu.make_async_copy(
            act.at[:, pl.ds(pl.multiple_of(c * BLK + p * PW, PW), PW)], abuf.at[0, mine, cols(p)], aloc.at[p])

    def mate_a(p):
        return remote(
            act.at[:, pl.ds(pl.multiple_of((1 - c) * BLK + p * PW, PW), PW)], abuf.at[0, mine, cols(p)],
            ad2d_s.at[p], ad2d_r.at[p], mate)

    for p in range(NP):
        mate_a(p).start()
        local_a(p).start()
    g_local = pltpu.make_async_copy(og, gbuf.at[mine, own_cols], gloc)
    g_beside = remote(og, gbuf.at[mine, own_cols], gs.at[0], gr.at[0], beside)
    g_mate = remote(og, gbuf.at[mine, own_cols], gs.at[1], gr.at[1], mate)
    g_pass = remote(gbuf.at[mine, other_cols], gbuf.at[mine, other_cols], gs.at[2], gr.at[2], mate)
    g_local.start()
    g_beside.start()
    g_mate.start()

    def send_up(p):
        return remote(abuf.at[0, :, cols(p)], abuf.at[3, :, cols(p)], ys.at[0, p], yr.at[0, p], up)

    def send_down(p):
        return remote(abuf.at[0, :, cols(p)], abuf.at[1, :, cols(p)], ys.at[1, p], yr.at[1, p], down)

    def pass_down(p):
        return remote(
            abuf.at[1, 0:TOK, cols(p)], abuf.at[2, 0:TOK, cols(p)], ws.at[0, p], wr.at[0, p], down)

    def pass_up(p):
        return remote(
            abuf.at[3, TOK : 2 * TOK, cols(p)], abuf.at[2, TOK : 2 * TOK, cols(p)], ws.at[1, p], wr.at[1, p], up)

    def ready(p):
        local_a(p).wait()
        mate_a(p).wait_recv()

    for p in range(NP):
        ready(p)
        if p < 1:
            send_up(p).start()
            send_down(p).start()

    def factor_rows(p, carry):
        fs[cols(p), :] = contract0(abuf[0, :, cols(p)], abuf[0])
        return carry

    lax.fori_loop(0, NP, factor_rows, 0)
    fbuf[:, 48:64, :] = jnp.zeros((16, 16, BLK), bf16)

    def strips(r, carry):
        fbuf[r, 0:56, :] = fs[pl.ds(pl.multiple_of(r * 56, 8), 56), :].astype(bf16)
        return carry

    lax.fori_loop(0, 16, strips, 0)
    basis = pltpu.make_async_copy(basis_in.at[0], fs, qloc)
    basis.start()
    r1[...] = jnp.zeros_like(r1)
    g_local.wait()
    g_here = gbuf[mine, own_cols]
    obuf[...] = contract0(g_here, g_here).astype(bf16)

    theirs, ours = (1 - xh) * 8, xh * 8
    swap = (
        remote(fbuf.at[pl.ds(theirs, 8)], fswap, fss.at[0], frs.at[0], across),
        remote(obuf.at[pl.ds(pl.multiple_of(theirs * 32, 256), 256), :], oswap, oss.at[0], ors.at[0], across),
    )
    def strip(dz, cc):
        return ((z + dz) % 4) * 2 + (c + cc) % 2

    def send_strip(k):
        dz, cc = column[k - 1]
        to = device(xh, xl, y, z + dz, (c + cc) % 2)
        r = strip(dz, cc)
        return (
            remote(fswap.at[r], frecv.at[k], fss.at[k], frs.at[k], to),
            remote(oswap.at[pl.ds(pl.multiple_of(r * 32, 32), 32), :], orecv.at[k], oss.at[k], ors.at[k], to),
        )

    def send_strips():
        for copy in swap:
            copy.wait_recv()

        def add(r, carry):
            fswap[r] = (fswap[r].astype(f32) + fbuf[ours + r].astype(f32)).astype(bf16)
            return carry

        lax.fori_loop(0, 8, add, 0)
        oswap[...] = (oswap[...].astype(f32)
                      + obuf[pl.ds(pl.multiple_of(ours * 32, 256), 256), :].astype(f32)).astype(bf16)
        for k in range(1, 8):
            for copy in send_strip(k):
                copy.start()

    def partial(d, p, tx):
        e = (y - z + d + 4) % 4
        other = gbuf[:, pl.ds(pl.multiple_of(tx * ROWS, ROWS), ROWS)]
        pbuf[e, tx, cols(p), :] = contract0(abuf[d, :, cols(p)], other).astype(bf16)

    def hop1(p, tx):
        near = pl.ds(pl.multiple_of(p * PW, 64), 64)
        far = pl.ds(pl.multiple_of(p * PW + 64, 64), 64)
        rows = pl.ds(pl.multiple_of(p * 64, 64), 64)
        return (
            remote(pbuf.at[2, tx, near, :], h1.at[0, tx, rows, :], h1s.at[0, p, tx], h1r.at[0, p, tx], fore),
            remote(pbuf.at[2, tx, far, :], h1.at[1, tx, rows, :], h1s.at[1, p, tx], h1r.at[1, p, tx], back),
        )

    def hop2(p, tx):
        return (
            remote(pbuf.at[1, tx, cols(p), :], h2.at[0, tx, cols(p), :], h2s.at[0, p, tx], h2r.at[0, p, tx], fore),
            remote(pbuf.at[3, tx, cols(p), :], h2.at[1, tx, cols(p), :], h2s.at[1, p, tx], h2r.at[1, p, tx], back),
        )

    def add_hop1(p, tx):
        near = pl.ds(pl.multiple_of(p * PW, 64), 64)
        far = pl.ds(pl.multiple_of(p * PW + 64, 64), 64)
        rows = pl.ds(pl.multiple_of(p * 64, 64), 64)
        pbuf[1, tx, near, :] = (pbuf[1, tx, near, :].astype(f32) + h1[0, tx, rows, :].astype(f32)).astype(bf16)
        pbuf[3, tx, far, :] = (pbuf[3, tx, far, :].astype(f32) + h1[1, tx, rows, :].astype(f32)).astype(bf16)

    def to_owner(tx, p):
        return remote(
            sbuf.at[tx, cols(p), :], xr.at[xh, cols(p), :], xs.at[tx, p], xrs.at[xh, p], device(xl, tx, y, z, c))

    def from_half(kx, p):
        return remote(
            sbuf.at[0, cols(p), :], xr.at[kx, cols(p), :], xs.at[0, p], xrs.at[kx, p], beside)

    def is_self(tx):
        return jnp.logical_and(xh == xl, xl == tx)

    def comes_from_self(kx):
        return jnp.logical_and(xh == xl, kx == xh)

    own, oth = xl, 1 - xl

    def near_tail(p, tx):
        pass_down(p).wait_recv()
        pass_up(p).wait_recv()
        partial(2, p, tx)
        for copy in hop1(p, tx):
            copy.start()

    def step(i, carry):
        @pl.when(jnp.logical_and(i >= LAG2, i < NP + LAG2))
        def _():
            p = i - LAG2
            for tx in (own, oth):
                for copy in hop1(p, tx):
                    copy.wait_recv()
                add_hop1(p, tx)
                for copy in hop2(p, tx):
                    copy.start()

        @pl.when(i == 2)
        def _():
            basis.wait()

            def halves(p, carry):
                high, low = split(fs[cols(p), :])
                qh[cols(p), :] = high
                ql[cols(p), :] = low
                return carry

            lax.fori_loop(0, NP, halves, 0)

        @pl.when(i == STRIPS)
        def _():
            send_strips()

        @pl.when(i < NP)
        def _():
            @pl.when(i + 1 < NP)
            def _():
                send_up(i).wait_send()
                send_down(i).wait_send()
                send_up(i + 1).start()
                send_down(i + 1).start()

            send_down(i).wait_recv()
            pass_down(i).start()
            send_up(i).wait_recv()
            pass_up(i).start()

            @pl.when(i == 0)
            def _():
                g_mate.wait_recv()

            for d in (0, 1, 3):
                partial(d, i, own)

            @pl.when(i == 1)
            def _():
                g_pass.wait_recv()
                for d in (0, 1, 3):
                    partial(d, 0, oth)

            @pl.when(i >= 1)
            def _():
                for d in (0, 1, 3):
                    partial(d, i, oth)

            @pl.when(i == 0)
            def _():
                near_tail(0, own)
                g_beside.wait_recv()
                g_pass.start()
                for copy in swap:
                    copy.start()

        @pl.when(jnp.logical_and(i >= 1, i < NP + 1))
        def _():
            p = i - 1

            @pl.when(i > 1)
            def _():
                near_tail(p, own)

            partial(2, p, oth)
            for copy in hop1(p, oth):
                copy.start()

        @pl.when(jnp.logical_and(i >= LAG3, i < NP + LAG3))
        def _():
            p = i - LAG3
            for tx in range(2):
                for copy in hop2(p, tx):
                    copy.wait_recv()
                total = (pbuf[0, tx, cols(p), :].astype(f32) + h2[0, tx, cols(p), :].astype(f32)
                         + h2[1, tx, cols(p), :].astype(f32))
                sbuf[tx, cols(p), :] = total.astype(bf16)

                @pl.when(is_self(tx))
                def _():
                    xr[xh, cols(p), :] = total.astype(bf16)

                @pl.when(jnp.logical_not(is_self(tx)))
                def _():
                    to_owner(tx, p).start()

        @pl.when(i >= LAG4)
        def _():
            p = i - LAG4
            for kx in range(2):
                @pl.when(jnp.logical_not(comes_from_self(kx)))
                def _():
                    from_half(kx, p).wait_recv()
            high, low = split((xr[0, cols(p), :].astype(f32) + xr[1, cols(p), :].astype(f32)) * SCALE)
            left = jnp.concatenate([qh[cols(p), :], ql[cols(p), :], qh[cols(p), :]], axis=0)
            right = jnp.concatenate([high, high, low], axis=0)
            r1[...] += contract0(left, right)

        return carry

    lax.fori_loop(0, NP + LAG4, step, 0)

    oh, ol = split(basis_out[...])
    for start, size in (FIRST, LAST):
        rows = slice(start, start + size)
        mh, ml = split(r1[rows, :])
        turned = dot(mh, oh) + dot(mh, ol) + dot(ml, oh)
        for p in range(start // 128, (start + size) // 128):
            spread = jnp.transpose(jnp.broadcast_to(eigen_in[p : p + 1, :], (128, 128)))
            for k in range(ROWS // 128):
                lanes = slice(k * 128, (k + 1) * 128)
                scaled = turned[p * 128 - start : (p + 1) * 128 - start, lanes] / (
                    spread * eigen_out[:, lanes] + damping)
                vbuf[p * 128 : (p + 1) * 128, lanes] = scaled.astype(bf16)
        back_out = lax.dot_general(
            vbuf[rows, :], oh, (((1,), (1,)), ((), ())), preferred_element_type=f32)
        vbuf[rows, :] = back_out.astype(bf16)

    def part(other, dz, core, start, size):
        half = (1 - xh) if other else xh
        base = (half * 8 + ((z + dz) % 4) * 2 + core) * BLK
        return u.at[pl.ds(pl.multiple_of(base + start, 64), size), :]

    def hand(other, dz, start, size, ssem, rsem, to):
        return remote(part(other, dz, c, start, size), part(other, dz, c, start, size), ssem, rsem, to)

    waits = []

    def go(descriptor):
        descriptor.start()
        waits.append(descriptor)
        return descriptor

    def ring(sem, other, start, size):
        go(hand(other, 0, start, size, zs.at[0, sem], zr.at[0, sem], fore))
        go(hand(other, 0, start, size, zs.at[1, sem], zr.at[1, sem], back))

    def ring_take(sem, other, start, size):
        hand(other, 3, start, size, zs.at[0, sem], zr.at[0, sem], fore).wait_recv()
        hand(other, 1, start, size, zs.at[1, sem], zr.at[1, sem], back).wait_recv()

    def relay(sem, other, start, size):
        half = size // 2
        go(hand(other, 3, start, half, vs.at[0, sem], vr.at[0, sem], fore))
        go(hand(other, 1, start + half, half, vs.at[1, sem], vr.at[1, sem], back))

    def relay_take(sem, other, start, size):
        half = size // 2
        hand(other, 2, start, half, vs.at[0, sem], vr.at[0, sem], fore).wait_recv()
        hand(other, 2, start + half, half, vs.at[1, sem], vr.at[1, sem], back).wait_recv()

    def cross(sem, dz, start, size):
        go(hand(False, dz, start, size, cs.at[sem], cr.at[sem], across))

    def cross_take(sem, dz, start, size):
        hand(True, dz, start, size, cs.at[sem], cr.at[sem], across).wait_recv()

    given = []

    def share(other, dz, start, size):
        sem = len(given)
        go(hand(other, dz, start, size, ds.at[sem], dr.at[sem], mate))
        given.append((other, dz, start, size))

    for k, (start, size) in enumerate(PARTS):
        block = dot(qh[start : start + size, :], vbuf[...]).astype(bf16)
        u[pl.ds(pl.multiple_of(me * BLK + start, 64), size), :] = block
        if k < 2:
            cross(k, 0, start, size)
            ring(k, False, start, size)
        if k == 3:
            ring(2, False, *LAST)
            cross(2, 0, *LAST)
    share(False, 0, *FIRST)
    share(False, 0, *LAST)
    for k in range(1, 8):
        for copy in send_strip(k):
            copy.wait_recv()
    here = fswap[z * 2 + c, 0:56, :].astype(f32)
    for k in range(1, 4):
        here += frecv[k, 0:56, :].astype(f32)
    there = frecv[4, 0:56, :].astype(f32)
    for k in range(5, 8):
        there += frecv[k, 0:56, :].astype(f32)
    fin_out[c] = here * SCALE
    fin_out[1 - c] = there * SCALE
    total = oswap[pl.ds(pl.multiple_of((z * 2 + c) * 32, 32), 32), :].astype(f32)
    for k in range(1, 8):
        total += orecv[k].astype(f32)
    fout_out[...] = total * SCALE

    for k in range(2):
        ring_take(k, False, *PARTS[k])
        relay(k, False, *PARTS[k])
    for k in range(2):
        cross_take(k, 0, *PARTS[k])
        ring(3 + k, True, *PARTS[k])
    ring_take(2, False, *LAST)
    relay(2, False, *LAST)
    cross(3, 1, *LAST)
    cross(4, 3, *LAST)
    for dz in (1, 3):
        share(False, dz, 0, BLK)
    share(True, 0, *FIRST)
    for k in range(2):
        relay_take(k, False, *PARTS[k])
    share(False, 2, *FIRST)
    relay_take(2, False, *LAST)
    cross(5, 2, *LAST)
    share(False, 2, *LAST)
    cross_take(2, 0, *LAST)
    share(True, 0, *LAST)
    for k in range(2):
        ring_take(3 + k, True, *PARTS[k])
        relay(3 + k, True, *PARTS[k])
    share(True, 1, *FIRST)
    share(True, 3, *FIRST)
    cross_take(3, 1, *LAST)
    share(True, 1, *LAST)
    cross_take(4, 3, *LAST)
    share(True, 3, *LAST)
    cross_take(5, 2, *LAST)
    share(True, 2, *LAST)
    for k in range(2):
        relay_take(3 + k, True, *PARTS[k])
        share(True, 2, *PARTS[k])
    for sem, (other, dz, start, size) in enumerate(given):
        ref = part(other, dz, 1 - c, start, size)
        remote(ref, ref, ds.at[sem], dr.at[sem], mate).wait_recv()
    for descriptor in waits:
        descriptor.wait_send()

    for copy in (g_beside, g_mate, g_pass):
        copy.wait_send()

    def finish(p, carry):
        mate_a(p).wait_send()
        for copy in (pass_down(p), pass_up(p)):
            copy.wait_send()
        for tx in range(2):
            for copy in hop1(p, tx) + hop2(p, tx):
                copy.wait_send()

            @pl.when(jnp.logical_not(is_self(tx)))
            def _():
                to_owner(tx, p).wait_send()
        return carry

    lax.fori_loop(0, NP, finish, 0)
    for p in range(NP - 1, NP):
        send_up(p).wait_send()
        send_down(p).wait_send()

    for copy in swap:
        copy.wait_send()
    for k in range(1, 8):
        for copy in send_strip(k):
            copy.wait_send()


def whole_step(activations, output_grads, basis_in, eigen_in, basis_out, eigen_out):
    dma = pltpu.SemaphoreType.DMA
    any_spec = pl.BlockSpec(memory_space=pl.ANY)
    vmem = pl.BlockSpec(memory_space=pltpu.VMEM)
    return pl.pallas_call(
        step_kernel,
        out_shape=(
            pltpu.VMEM((16 * BLK, ROWS), bf16),
            jax.ShapeDtypeStruct((2, 56, BLK), f32),
            jax.ShapeDtypeStruct((32, ROWS), f32),
        ),
        in_specs=[any_spec, any_spec, any_spec, vmem, vmem, vmem],
        out_specs=(vmem, vmem, vmem),
        scratch_shapes=[
            pltpu.VMEM((4, 2 * TOK, BLK), bf16),
            pltpu.VMEM((2 * TOK, 2 * ROWS), bf16),
            pltpu.VMEM((4, 2, BLK, ROWS), bf16),
            pltpu.VMEM((2, 2, BLK // 2, ROWS), bf16),
            pltpu.VMEM((2, 2, BLK, ROWS), bf16),
            pltpu.VMEM((2, BLK, ROWS), bf16),
            pltpu.VMEM((2, BLK, ROWS), bf16),
            pltpu.VMEM((BLK, BLK), f32),
            pltpu.VMEM((16, 64, BLK), bf16),
            pltpu.VMEM((8, 64, BLK), bf16),
            pltpu.VMEM((8, 64, BLK), bf16),
            pltpu.VMEM((ROWS, ROWS), bf16),
            pltpu.VMEM((ROWS // 2, ROWS), bf16),
            pltpu.VMEM((8, 32, ROWS), bf16),
            dma((NP,)), dma((NP,)), dma((NP,)),
            dma, dma((3,)), dma((3,)),
            dma((2, NP)), dma((2, NP)), dma((2, NP)), dma((2, NP)),
            dma((2, NP, 2)), dma((2, NP, 2)), dma((2, NP, 2)), dma((2, NP, 2)),
            dma((2, NP)), dma((2, NP)),
            dma((8,)), dma((8,)), dma((8,)), dma((8,)),
            pltpu.VMEM((BLK, BLK), bf16),
            pltpu.VMEM((BLK, BLK), bf16),
            pltpu.VMEM((BLK, ROWS), f32),
            pltpu.VMEM((BLK, ROWS), bf16),
            dma,
            dma((2, 5)), dma((2, 5)), dma((2, 5)), dma((2, 5)),
            dma((6,)), dma((6,)), dma((20,)), dma((20,)),
        ],
        compiler_params=pltpu.CompilerParams(
            collective_id=0, has_side_effects=True, vmem_limit_bytes=48 * 2**20),
        cost_estimate=pl.CostEstimate(flops=15_000_000_000, bytes_accessed=26_000_000, transcendentals=0),
        name="kfac_step",
    )(activations, output_grads, basis_in, eigen_in, basis_out, eigen_out)


def body(activations, output_grads, basis_in, eigen_in, basis_out, eigen_out):
    update, fin, factor_out = whole_step(
        activations, output_grads, basis_in, eigen_in.reshape(NP, PW), basis_out, eigen_out.reshape(1, ROWS))
    return (update, jnp.transpose(fin, (1, 0, 2)), factor_out)


def solution(mesh):
    in_specs = (
        P("dp", "tensor"),
        P("dp", "tensor"),
        P("dp", None, None),
        P("dp"),
        P("tensor", None),
        P("tensor"),
    )
    out_specs = (P(None, "tensor"), P("dp", "tensor", None), P("dp", "tensor"))
    return jax.shard_map(body, mesh=mesh, in_specs=in_specs, out_specs=out_specs, check_vma=False)
```

time: 290 us -> 171 us (0.59)
  waiting for transfers between devices: 101 us -> 0 us
  Pallas kernels: 126 us -> 164 us
  matrix products: 31.1 us -> 0 us
  between operations: 14.1 us -> 0.66 us
  local copies, waits for them, and re-layouts: 16.9 us -> 7.06 us
    all_gather x1 -> x0, waiting for transfers between devices: 101 us -> none  [body(): update = lax.all_gather(worker_slab, 'dp', axis=0, tiled=True)]
    pallas_call x1, Pallas kernels: 126 us -> 164 us  [whole_step(): pl.pallas_call(step_kernel, out_shape=(pltpu.VMEM((16 * BLK, ROWS), bf16)...]
    dot_general x4 -> x0, matrix products: 31.1 us -> none  [the longest x1 12.2 us: body(): back = jnp.einsum('bjl,bij->bil', scaled, basis_in, precision=highest)]
    unnamed x15 -> x7, local copies, waits for them, and re-layouts: 16.9 us -> 7.06 us
  transfers between devices with their start and end apart: 1 -> 0, of which waited for: 1 -> 0; matrix products, arithmetic and copies ran while one was open for 1% -> 0% of each run, Pallas kernels for 0% -> 0%
where the time goes in v3:
time: 171 us
  Pallas kernels  164 us (96%)
  local copies, waits for them, and re-layouts  7.06 us (4%)
    pallas_call x1, Pallas kernels, whole_step(): pl.pallas_call(step_kernel, out_shape=(pltpu.VMEM((16 * BLK, ROWS), bf16)...  164 us
    unnamed x7, local copies, waits for them, and re-layouts  7.06 us

profile of v3, /device:TPU:1, one launch (start us, length us, event | category | flops | bytes accessed | tf_op | source)
XLA Modules:
  0.0 171.2 jit_solution(7566327614129441591)
XLA Ops:
  0.6 163.5 %kfac_step.1 = (bf16[14336,512]{1,0:T(8,128)(2,1)S(1)}, f32[2,56,896]{2,1,0:T(8,128)}, f32[32,512]{1,0:T(8,128)}) custom-call(bf16[512,1792]{1,0:T(8,128)(2,1)} %act.1, bf16[512,512]{1,0:T(8,128)(2,1)} %og.1, f32[1,896,896]{2,1,0:T(8,128)} %basis_in.1, f32[7,128]{1,0:T(8,128)} %bitcast.4, f32[512,512]{1,0:T(8,128)} %basis_out.1, f32[1,512]{1,0:T(1,128)} %bitcast.5), custom_call_target="tpu_custom_call" | custom-call | flops 15000000512 | bytes 26000000 | tf_op jit(solution)/shard_map/kfac_step/pallas_call | solution.py:506
  164.1 0.0 copy-start
  164.2 0.0 copy-start.1
  164.2 5.5 %copy.12 = bf16[14336,512]{1,0:T(8,128)(2,1)} copy(bf16[14336,512]{1,0:T(8,128)(2,1)S(1)} %get-tuple-element.12) | data formatting | bytes 29360128
  169.6 0.0 copy-done
  169.6 1.0 copy.9
  170.6 0.0 copy-done.1
  170.6 0.6 copy.13
Async XLA Ops:
  164.1 5.5 %copy-start = (f32[2,56,896]{2,1,0:T(8,128)S(1)}, f32[2,56,896]{2,1,0:T(8,128)}, u32[]{:S(2)}) copy-start(f32[2,56,896]{2,1,0:T(8,128)} %get-tuple-element.7) | copy-start | bytes 1204228
  164.2 6.4 %copy-start.1 = (f32[32,512]{1,0:T(8,128)S(1)}, f32[32,512]{1,0:T(8,128)}, u32[]{:S(2)}) copy-start(f32[32,512]{1,0:T(8,128)} %get-tuple-element.20) | copy-start | bytes 196612

commit v4 on v3

--- a/solution.py
+++ b/solution.py
@@ -13,8 +13,9 @@
 NP = 7
 PW = 128
 SCALE = 1.0 / 8192
-LAG2, LAG3, LAG4 = 2, 3, 4
-STRIPS = NP + 1
+LAG2, LAG3, LAG4 = 2, 3, 6
+STRIPS = NP - 1 + LAG2
+AHEAD, RELAYS = 1, 1
 damping = 0.01
 f32, bf16 = jnp.float32, jnp.bfloat16
 
@@ -103,29 +104,39 @@
     g_beside.start()
     g_mate.start()
 
-    def send_up(p):
-        return remote(abuf.at[0, :, cols(p)], abuf.at[3, :, cols(p)], ys.at[0, p], yr.at[0, p], up)
-
-    def send_down(p):
-        return remote(abuf.at[0, :, cols(p)], abuf.at[1, :, cols(p)], ys.at[1, p], yr.at[1, p], down)
-
-    def pass_down(p):
-        return remote(
-            abuf.at[1, 0:TOK, cols(p)], abuf.at[2, 0:TOK, cols(p)], ws.at[0, p], wr.at[0, p], down)
-
-    def pass_up(p):
-        return remote(
-            abuf.at[3, TOK : 2 * TOK, cols(p)], abuf.at[2, TOK : 2 * TOK, cols(p)], ws.at[1, p], wr.at[1, p], up)
-
-    def ready(p):
+    theirs_too = pl.ds(pl.multiple_of((1 - c) * TOK, TOK), TOK)
+
+    def rounds(p):
+        out = []
+        for k, rows in enumerate((mine, theirs_too)):
+            out.append(remote(
+                abuf.at[0, rows, cols(p)], abuf.at[3, rows, cols(p)], ys.at[0, p, k], yr.at[0, p, k], up))
+            out.append(remote(
+                abuf.at[0, rows, cols(p)], abuf.at[1, rows, cols(p)], ys.at[1, p, k], yr.at[1, p, k], down))
+        return tuple(out)
+
+    def relays(p, first, second):
+        out = []
+        for k in range(RELAYS):
+            size = TOK // RELAYS
+            low, high = pl.ds(k * size, size), pl.ds(TOK + k * size, size)
+            if first:
+                out.append(remote(
+                    abuf.at[1, low, cols(p)], abuf.at[2, low, cols(p)], ws.at[0, p, k], wr.at[0, p, k], down))
+            if second:
+                out.append(remote(
+                    abuf.at[3, high, cols(p)], abuf.at[2, high, cols(p)], ws.at[1, p, k], wr.at[1, p, k], up))
+        return tuple(out)
+
+    for p in range(NP):
         local_a(p).wait()
+        if p == 0:
+            for copy in rounds(p)[:2]:
+                copy.start()
         mate_a(p).wait_recv()
-
-    for p in range(NP):
-        ready(p)
-        if p < 1:
-            send_up(p).start()
-            send_down(p).start()
+        if p < AHEAD:
+            for copy in rounds(p)[2 * (p == 0):]:
+                copy.start()
 
     def factor_rows(p, carry):
         fs[cols(p), :] = contract0(abuf[0, :, cols(p)], abuf[0])
@@ -221,12 +232,18 @@
 
     own, oth = xl, 1 - xl
 
+    def product(d, p, tx):
+        partial(d, p, tx)
+
+        @pl.when((y - z + d + 4) % 4 == 2)
+        def _():
+            for copy in hop1(p, tx):
+                copy.start()
+
     def near_tail(p, tx):
-        pass_down(p).wait_recv()
-        pass_up(p).wait_recv()
-        partial(2, p, tx)
-        for copy in hop1(p, tx):
-            copy.start()
+        for copy in relays(p, True, True):
+            copy.wait_recv()
+        product(2, p, tx)
 
     def step(i, carry):
         @pl.when(jnp.logical_and(i >= LAG2, i < NP + LAG2))
@@ -239,61 +256,50 @@
                 for copy in hop2(p, tx):
                     copy.start()
 
-        @pl.when(i == 2)
-        def _():
-            basis.wait()
-
-            def halves(p, carry):
-                high, low = split(fs[cols(p), :])
-                qh[cols(p), :] = high
-                ql[cols(p), :] = low
-                return carry
-
-            lax.fori_loop(0, NP, halves, 0)
-
-        @pl.when(i == STRIPS)
-        def _():
-            send_strips()
-
         @pl.when(i < NP)
         def _():
-            @pl.when(i + 1 < NP)
-            def _():
-                send_up(i).wait_send()
-                send_down(i).wait_send()
-                send_up(i + 1).start()
-                send_down(i + 1).start()
-
-            send_down(i).wait_recv()
-            pass_down(i).start()
-            send_up(i).wait_recv()
-            pass_up(i).start()
+            @pl.when(i + AHEAD < NP)
+            def _():
+                for copy in rounds(i):
+                    copy.wait_send()
+                for copy in rounds(i + AHEAD):
+                    copy.start()
+
+            arrivals = rounds(i)
+            for k in (1, 3):
+                arrivals[k].wait_recv()
+            for copy in relays(i, True, False):
+                copy.start()
+            for k in (0, 2):
+                arrivals[k].wait_recv()
+            for copy in relays(i, False, True):
+                copy.start()
 
             @pl.when(i == 0)
             def _():
                 g_mate.wait_recv()
 
             for d in (0, 1, 3):
-                partial(d, i, own)
+                product(d, i, own)
 
             @pl.when(i == 1)
             def _():
                 g_pass.wait_recv()
                 for d in (0, 1, 3):
-                    partial(d, 0, oth)
+                    product(d, 0, oth)
 
             @pl.when(i >= 1)
             def _():
                 for d in (0, 1, 3):
-                    partial(d, i, oth)
+                    product(d, i, oth)
 
             @pl.when(i == 0)
             def _():
-                near_tail(0, own)
                 g_beside.wait_recv()
                 g_pass.start()
                 for copy in swap:
                     copy.start()
+                near_tail(0, own)
 
         @pl.when(jnp.logical_and(i >= 1, i < NP + 1))
         def _():
@@ -303,9 +309,7 @@
             def _():
                 near_tail(p, own)
 
-            partial(2, p, oth)
-            for copy in hop1(p, oth):
-                copy.start()
+            product(2, p, oth)
 
         @pl.when(jnp.logical_and(i >= LAG3, i < NP + LAG3))
         def _():
@@ -324,6 +328,22 @@
                 @pl.when(jnp.logical_not(is_self(tx)))
                 def _():
                     to_owner(tx, p).start()
+
+        @pl.when(i == 2)
+        def _():
+            basis.wait()
+
+            def halves(p, carry):
+                high, low = split(fs[cols(p), :])
+                qh[cols(p), :] = high
+                ql[cols(p), :] = low
+                return carry
+
+            lax.fori_loop(0, NP, halves, 0)
+
+        @pl.when(i == STRIPS)
+        def _():
+            send_strips()
 
         @pl.when(i >= LAG4)
         def _():
@@ -414,22 +434,6 @@
             cross(2, 0, *LAST)
     share(False, 0, *FIRST)
     share(False, 0, *LAST)
-    for k in range(1, 8):
-        for copy in send_strip(k):
-            copy.wait_recv()
-    here = fswap[z * 2 + c, 0:56, :].astype(f32)
-    for k in range(1, 4):
-        here += frecv[k, 0:56, :].astype(f32)
-    there = frecv[4, 0:56, :].astype(f32)
-    for k in range(5, 8):
-        there += frecv[k, 0:56, :].astype(f32)
-    fin_out[c] = here * SCALE
-    fin_out[1 - c] = there * SCALE
-    total = oswap[pl.ds(pl.multiple_of((z * 2 + c) * 32, 32), 32), :].astype(f32)
-    for k in range(1, 8):
-        total += orecv[k].astype(f32)
-    fout_out[...] = total * SCALE
-
     for k in range(2):
         ring_take(k, False, *PARTS[k])
         relay(k, False, *PARTS[k])
@@ -465,6 +469,22 @@
     for k in range(2):
         relay_take(3 + k, True, *PARTS[k])
         share(True, 2, *PARTS[k])
+    for k in range(1, 8):
+        for copy in send_strip(k):
+            copy.wait_recv()
+    here = fswap[z * 2 + c, 0:56, :].astype(f32)
+    for k in range(1, 4):
+        here += frecv[k, 0:56, :].astype(f32)
+    there = frecv[4, 0:56, :].astype(f32)
+    for k in range(5, 8):
+        there += frecv[k, 0:56, :].astype(f32)
+    fin_out[c] = here * SCALE
+    fin_out[1 - c] = there * SCALE
+    total = oswap[pl.ds(pl.multiple_of((z * 2 + c) * 32, 32), 32), :].astype(f32)
+    for k in range(1, 8):
+        total += orecv[k].astype(f32)
+    fout_out[...] = total * SCALE
+
     for sem, (other, dz, start, size) in enumerate(given):
         ref = part(other, dz, 1 - c, start, size)
         remote(ref, ref, ds.at[sem], dr.at[sem], mate).wait_recv()
@@ -476,7 +496,7 @@
 
     def finish(p, carry):
         mate_a(p).wait_send()
-        for copy in (pass_down(p), pass_up(p)):
+        for copy in relays(p, True, True):
             copy.wait_send()
         for tx in range(2):
             for copy in hop1(p, tx) + hop2(p, tx):
@@ -488,9 +508,9 @@
         return carry
 
     lax.fori_loop(0, NP, finish, 0)
-    for p in range(NP - 1, NP):
-        send_up(p).wait_send()
-        send_down(p).wait_send()
+    for p in range(NP - AHEAD, NP):
+        for copy in rounds(p):
+            copy.wait_send()
 
     for copy in swap:
         copy.wait_send()
@@ -529,7 +549,7 @@
             pltpu.VMEM((8, 32, ROWS), bf16),
             dma((NP,)), dma((NP,)), dma((NP,)),
             dma, dma((3,)), dma((3,)),
-            dma((2, NP)), dma((2, NP)), dma((2, NP)), dma((2, NP)),
+            dma((2, NP, 2)), dma((2, NP, 2)), dma((2, NP, RELAYS)), dma((2, NP, RELAYS)),
             dma((2, NP, 2)), dma((2, NP, 2)), dma((2, NP, 2)), dma((2, NP, 2)),
             dma((2, NP)), dma((2, NP)),
             dma((8,)), dma((8,)), dma((8,)), dma((8,)),

time: 171 us -> 168 us (0.982)
  Pallas kernels: 164 us -> 160 us
    pallas_call x1, Pallas kernels: 164 us -> 160 us  [whole_step(): pl.pallas_call(step_kernel, out_shape=(pltpu.VMEM((16 * BLK, ROWS), bf16)...]
where the time goes in v4:
time: 168 us
  Pallas kernels  160 us (95%)
  local copies, waits for them, and re-layouts  7.06 us (4%)
    pallas_call x1, Pallas kernels, whole_step(): pl.pallas_call(step_kernel, out_shape=(pltpu.VMEM((16 * BLK, ROWS), bf16)...  160 us
    unnamed x7, local copies, waits for them, and re-layouts  7.06 us

profile of v4, /device:TPU:1, one launch (start us, length us, event | category | flops | bytes accessed | tf_op | source)
XLA Modules:
  0.0 167.7 jit_solution(13974147412120209456)
XLA Ops:
  0.6 159.9 %kfac_step.1 = (bf16[14336,512]{1,0:T(8,128)(2,1)S(1)}, f32[2,56,896]{2,1,0:T(8,128)}, f32[32,512]{1,0:T(8,128)}) custom-call(bf16[512,1792]{1,0:T(8,128)(2,1)} %act.1, bf16[512,512]{1,0:T(8,128)(2,1)} %og.1, f32[1,896,896]{2,1,0:T(8,128)} %basis_in.1, f32[7,128]{1,0:T(8,128)} %bitcast.4, f32[512,512]{1,0:T(8,128)} %basis_out.1, f32[1,512]{1,0:T(1,128)} %bitcast.5), custom_call_target="tpu_custom_call" | custom-call | flops 15000000512 | bytes 26000000 | tf_op jit(solution)/shard_map/kfac_step/pallas_call | solution.py:526
  160.6 0.0 copy-start
  160.6 0.0 copy-start.1
  160.6 5.5 %copy.12 = bf16[14336,512]{1,0:T(8,128)(2,1)} copy(bf16[14336,512]{1,0:T(8,128)(2,1)S(1)} %get-tuple-element.12) | data formatting | bytes 29360128
  166.1 0.0 copy-done
  166.1 1.0 copy.9
  167.0 0.0 copy-done.1
  167.0 0.6 copy.13
Async XLA Ops:
  160.6 5.5 %copy-start = (f32[2,56,896]{2,1,0:T(8,128)S(1)}, f32[2,56,896]{2,1,0:T(8,128)}, u32[]{:S(2)}) copy-start(f32[2,56,896]{2,1,0:T(8,128)} %get-tuple-element.7) | copy-start | bytes 1204228
  160.6 6.4 %copy-start.1 = (f32[32,512]{1,0:T(8,128)S(1)}, f32[32,512]{1,0:T(8,128)}, u32[]{:S(2)}) copy-start(f32[32,512]{1,0:T(8,128)} %get-tuple-element.20) | copy-start | bytes 196612

commit v5 on v4

--- a/solution.py
+++ b/solution.py
@@ -246,6 +246,13 @@
         product(2, p, tx)
 
     def step(i, carry):
+        @pl.when(i + AHEAD < NP)
+        def _():
+            for copy in rounds(i):
+                copy.wait_send()
+            for copy in rounds(i + AHEAD):
+                copy.start()
+
         @pl.when(jnp.logical_and(i >= LAG2, i < NP + LAG2))
         def _():
             p = i - LAG2
@@ -258,13 +265,6 @@
 
         @pl.when(i < NP)
         def _():
-            @pl.when(i + AHEAD < NP)
-            def _():
-                for copy in rounds(i):
-                    copy.wait_send()
-                for copy in rounds(i + AHEAD):
-                    copy.start()
-
             arrivals = rounds(i)
             for k in (1, 3):
                 arrivals[k].wait_recv()

time: 168 us -> 167 us (level)
  no operation moved by 1% of the time
where the time goes in v5:
time: 167 us
  Pallas kernels  159 us (95%)
  local copies, waits for them, and re-layouts  7.06 us (4%)
    pallas_call x1, Pallas kernels, whole_step(): pl.pallas_call(step_kernel, out_shape=(pltpu.VMEM((16 * BLK, ROWS), bf16)...  159 us
    unnamed x7, local copies, waits for them, and re-layouts  7.06 us

profile of v5, /device:TPU:1, one launch (start us, length us, event | category | flops | bytes accessed | tf_op | source)
XLA Modules:
  0.0 167.1 jit_solution(1074126246609872416)
XLA Ops:
  0.6 159.4 %kfac_step.1 = (bf16[14336,512]{1,0:T(8,128)(2,1)S(1)}, f32[2,56,896]{2,1,0:T(8,128)}, f32[32,512]{1,0:T(8,128)}) custom-call(bf16[512,1792]{1,0:T(8,128)(2,1)} %act.1, bf16[512,512]{1,0:T(8,128)(2,1)} %og.1, f32[1,896,896]{2,1,0:T(8,128)} %basis_in.1, f32[7,128]{1,0:T(8,128)} %bitcast.4, f32[512,512]{1,0:T(8,128)} %basis_out.1, f32[1,512]{1,0:T(1,128)} %bitcast.5), custom_call_target="tpu_custom_call" | custom-call | flops 15000000512 | bytes 26000000 | tf_op jit(solution)/shard_map/kfac_step/pallas_call | solution.py:526
  160.0 0.0 copy-start
  160.0 0.0 copy-start.1
  160.0 5.5 %copy.12 = bf16[14336,512]{1,0:T(8,128)(2,1)} copy(bf16[14336,512]{1,0:T(8,128)(2,1)S(1)} %get-tuple-element.12) | data formatting | bytes 29360128
  165.5 0.0 copy-done
  165.5 1.0 copy.9
  166.5 0.0 copy-done.1
  166.5 0.6 copy.13
Async XLA Ops:
  160.0 5.5 %copy-start = (f32[2,56,896]{2,1,0:T(8,128)S(1)}, f32[2,56,896]{2,1,0:T(8,128)}, u32[]{:S(2)}) copy-start(f32[2,56,896]{2,1,0:T(8,128)} %get-tuple-element.7) | copy-start | bytes 1204228
  160.0 6.4 %copy-start.1 = (f32[32,512]{1,0:T(8,128)S(1)}, f32[32,512]{1,0:T(8,128)}, u32[]{:S(2)}) copy-start(f32[32,512]{1,0:T(8,128)} %get-tuple-element.20) | copy-start | bytes 196612
